TPU v7x, 32 devices: a whole 2x2x4 slice. The times are simulated.
32 devices in a mesh: groups: 2 (over x), tensor: 8 (over z, y), rep: 2 (over core).
Axes of the slice: x: 2, y: 2, z: 4, core: 2. Of those that a mesh axis runs over, the one named last changes fastest.
Arguments:
- acts: bfloat16 [3, 256, 8192], P(None, ('groups', 'rep'), 'tensor'), parts along dimension 1, may hold values from -6 to 6
- base_projection_weight: bfloat16 [8192, 8192], P(None, 'tensor'), may hold values from -0.0625 to 0.0625
- adapter_down_factors: bfloat16 [32, 8192, 64], P('tensor'), may hold values from -0.0625 to 0.0625
- adapter_up_factors: bfloat16 [32, 64, 8192], P('tensor'), may hold values from -0.75 to 0.75
- requested_adapter_ids: int32 [3, 256], P(None, ('groups', 'rep')), parts along dimension 1, may hold values from 0 to 31, as said below
- slot_of_adapter: int32 [64], P('groups'), parts along dimension 0, may hold values from 0 to 31, as said below
- active_row_counts: int32 [6], P('groups'), parts along dimension 0, may hold values from 32 to 64
Outputs:
- projected: bfloat16 [3, 256, 8192], P(None, ('groups', 'rep'), 'tensor'), parts along dimension 1
There are 2 independent parts, one for each index of `groups`. A program takes and returns all parts, laid end to end along the dimension named above; an argument that names none is the same for every part. Nothing has to cross between parts.
Inputs may be any that keep to these rules, and one draw needn't show every extreme that they name: `requested_adapter_ids`: for each step and each batch shard of 64 rows (rows r * 64 to (r + 1) * 64 - 1), the owner slot_of_adapter[id] // 4 of the rows' ids is the same for at most 16 rows, live or not, and for exactly 16 rows for some owner. `slot_of_adapter`: each slot number appears once.
All inputs are finite; a program needn't handle non-finite values.
Results may differ from a plain program's by a relative error of at most 0.0049.
Values may be sent and summed in bfloat16 or wider, within the bound.
A program may use at most 128 MiB of HBM per device.

v0:
```python
import functools

import jax
import jax.numpy as jnp
from jax import lax
from jax.experimental import pallas as pl
from jax.experimental.pallas import tpu as pltpu
from jax.sharding import PartitionSpec as P

CAP = 16
VMEM_LIMIT = 60 * 1024 * 1024


def grid_of(n):
    short = 1
    while (short * 2) * (short * 2) <= n:
        short *= 2
    return n // short, short


def position_of(index, n):
    long, short = grid_of(n)
    a, b = index // short, index % short
    inner = (b + short - 1) // short
    odd = a % 2
    snake = a * (short - 1) + (1 - odd) * (b - 1) + odd * (short - 1 - b)
    return inner * snake + (1 - inner) * (n - 1 - a)


def index_of(position, n):
    long, short = grid_of(n)
    back = position // (long * (short - 1))
    a = position // (short - 1)
    c = position % (short - 1)
    odd = a % 2
    b = 1 + (1 - odd) * c + odd * (short - 2 - c)
    return (1 - back) * (a * short + b) + back * ((n - 1 - position) * short)


def kernel(
    n,
    acts_ref,
    ids_ref,
    table_ref,
    counts_ref,
    w_hbm,
    down_hbm,
    up_hbm,
    out_ref,
    w_v,
    down_v,
    up_v,
    g,
    acc,
    low,
    scatter,
    d_send,
    d_recv,
    w_sem,
    down_sem,
    up_sem,
    g_send_sem,
    g_recv_sem,
    a_send_sem,
    a_recv_sem,
):
    steps, rows, width = acts_ref.shape
    holds, rank, _ = down_hbm.shape
    half = rows // 2
    hops = n // 2
    me = lax.axis_index("tensor")
    place = position_of(me, n)
    ring = (
        index_of((place + 1) % n, n),
        index_of((place + n - 1) % n, n),
    )

    def slot_of(direction, hop):
        return min(1 + direction + 2 * hop, n - 1)

    def origin(slot):
        hop = (slot + 1) // 2
        away = n - hop if slot % 2 == 1 else hop
        return index_of((place + away) % n, n)

    def w_copies(slot):
        at = pl.ds(pl.multiple_of(origin(slot) * width, width), width)
        return (
            pltpu.make_async_copy(w_hbm.at[at], w_v.at[slot], w_sem.at[slot]),
            pltpu.make_async_copy(
                down_hbm.at[:, :, at], down_v.at[slot], down_sem.at[slot]
            ),
        )

    up_copy = pltpu.make_async_copy(up_hbm, up_v, up_sem)

    for slot in range(n):
        for copy in w_copies(slot):
            copy.start()
    up_copy.start()

    barrier = pltpu.get_barrier_semaphore()

    def greet(offset, carry):
        pl.semaphore_signal(
            barrier,
            inc=1,
            device_id={"tensor": (me + offset) % n},
            device_id_type=pl.DeviceIdType.MESH,
        )
        return carry

    lax.fori_loop(1, n, greet, 0)
    pl.semaphore_wait(barrier, n - 1)

    def hop_copy(direction, s, hop, part):
        at = pl.ds(part * half, half)
        if hop == 0:
            src = acts_ref.at[s, at]
        else:
            src = g.at[s, slot_of(direction, hop - 1), at]
        return pltpu.make_async_remote_copy(
            src_ref=src,
            dst_ref=g.at[s, slot_of(direction, hop), at],
            send_sem=g_send_sem.at[s, direction, hop, part],
            recv_sem=g_recv_sem.at[s, direction, hop, part],
            device_id={"tensor": ring[direction]},
            device_id_type=pl.DeviceIdType.MESH,
        )

    def travels(direction, hop, part):
        return hop < hops - 1 or (hop == hops - 1 and part == direction)

    def start_first(s):
        for part in range(2):
            for direction in range(2):
                if travels(direction, 0, part):
                    hop_copy(direction, s, 0, part).start()

    def term_copy(s, offset):
        return pltpu.make_async_remote_copy(
            src_ref=d_send.at[s, offset],
            dst_ref=d_recv.at[s, pl.ds(pl.multiple_of(me * CAP, CAP), CAP)],
            send_sem=a_send_sem.at[s, offset],
            recv_sem=a_recv_sem.at[s, offset],
            device_id={"tensor": (me + offset) % n},
            device_id_type=pl.DeviceIdType.MESH,
        )

    def take_weights(s, slot):
        @pl.when(s == 0)
        def _():
            for copy in w_copies(slot):
                copy.wait()

    def add_product(s, slot, block):
        base = jnp.dot(block, w_v[slot], preferred_element_type=jnp.float32)
        small = lax.dot_general(
            block,
            down_v[slot].reshape(holds * rank, width),
            (((1,), (1,)), ((), ())),
            preferred_element_type=jnp.float32,
        )
        if slot == 0:
            acc[s] = base
            low[...] = small
        else:
            acc[s] += base
            low[...] += small

    f32 = jnp.float32

    def iota(shape, dim):
        return lax.broadcasted_iota(jnp.int32, shape, dim).astype(f32)

    def finish(s):
        def arrived(offset, carry):
            term_copy(s, offset).wait_recv()
            return carry

        lax.fori_loop(1, n, arrived, 0)
        delta = jnp.dot(scatter[s], d_recv[s], preferred_element_type=f32)
        out_ref[s] = (acc[s] + delta).astype(out_ref.dtype)

    start_first(0)

    def one_step(s, carry):
        take_weights(s, 0)
        add_product(s, 0, acts_ref[s])

        ids_row = ids_ref[pl.ds(s, 1), :].astype(f32)
        table = table_ref[...].astype(f32)
        down_at, across = iota((rows, rows), 0), iota((rows, rows), 1)
        eye = down_at == across
        ids_col = jnp.sum(jnp.where(eye, ids_row, 0.0), axis=1, keepdims=True)
        found = ids_col == iota((rows, table.shape[1]), 1)
        slot_col = jnp.sum(jnp.where(found, table, 0.0), axis=1, keepdims=True)
        owner_col = jnp.floor((slot_col + 0.5) * (1.0 / holds))
        local_col = slot_col - owner_col * holds
        owner_row = jnp.sum(jnp.where(eye, owner_col, 0.0), axis=0, keepdims=True)
        same = owner_col == owner_row
        rank_col = jnp.sum(
            jnp.where(same & (across < down_at), 1.0, 0.0), axis=1, keepdims=True
        )
        rank_row = jnp.sum(
            jnp.where(same & (down_at < across), 1.0, 0.0), axis=0, keepdims=True
        )
        alive = iota((rows, 1), 0) < counts_ref[s].astype(f32)
        target = jnp.where(alive, owner_col * CAP + rank_col, -1.0)
        scatter[s] = jnp.where(
            target == iota((rows, n * CAP), 1), 1.0, 0.0
        ).astype(jnp.bfloat16)
        pick = jnp.where(
            (rank_row == iota((CAP, rows), 0)) & (owner_row == me.astype(f32)), 1.0, 0.0
        ).astype(jnp.bfloat16)

        for hop in range(hops):
            if hop == max(hops - 2, 0):

                @pl.when(s + 1 < steps)
                def _():
                    start_first(s + 1)

            for part in range(2):
                for direction in range(2):
                    if travels(direction, hop, part):
                        hop_copy(direction, s, hop, part).wait_recv()
                        if travels(direction, hop + 1, part):
                            hop_copy(direction, s, hop + 1, part).start()
            for slot in sorted({slot_of(0, hop), slot_of(1, hop)}):
                take_weights(s, slot)
                add_product(s, slot, g[s, slot])

        held = lax.broadcasted_iota(jnp.int32, (rows, holds * rank), 1) // rank
        masked = jnp.where(local_col == held.astype(f32), low[...], 0.0)
        packed = jnp.dot(
            pick, masked.astype(jnp.bfloat16), preferred_element_type=f32
        ).astype(jnp.bfloat16)

        @pl.when(s == 0)
        def _():
            up_copy.wait()

        def term(device):
            at = pl.ds(pl.multiple_of(device * width, width), width)
            factor = up_v[:, :, at].reshape(holds * rank, width)
            return jnp.dot(packed, factor, preferred_element_type=f32).astype(
                jnp.bfloat16
            )

        def send_term(offset, carry):
            d_send[s, offset] = term((me + offset) % n)
            term_copy(s, offset).start()
            return carry

        lax.fori_loop(1, n, send_term, 0)
        d_recv[s, pl.ds(pl.multiple_of(me * CAP, CAP), CAP)] = term(me)

        @pl.when(s > 0)
        def _():
            finish(s - 1)

        return carry

    lax.fori_loop(0, steps, one_step, 0)
    finish(steps - 1)

    def drain(s, carry):
        for hop in range(hops):
            for part in range(2):
                for direction in range(2):
                    if travels(direction, hop, part):
                        hop_copy(direction, s, hop, part).wait_send()

        def sent(offset, inner):
            term_copy(s, offset).wait_send()
            return inner

        return lax.fori_loop(1, n, sent, carry)

    lax.fori_loop(0, steps, drain, 0)


def per_device(
    acts,
    base_projection_weight,
    adapter_down_factors,
    adapter_up_factors,
    requested_adapter_ids,
    slot_of_adapter,
    active_row_counts,
):
    n = lax.axis_size("tensor")
    steps, rows, width = acts.shape
    holds, full, rank = adapter_down_factors.shape
    bf16 = jnp.bfloat16
    hops = n // 2
    vmem = pl.BlockSpec(memory_space=pltpu.VMEM)
    anywhere = pl.BlockSpec(memory_space=pl.ANY)
    return pl.pallas_call(
        functools.partial(kernel, n),
        out_shape=jax.ShapeDtypeStruct(acts.shape, bf16),
        in_specs=[
            vmem,
            vmem,
            vmem,
            pl.BlockSpec(memory_space=pltpu.SMEM),
            anywhere,
            anywhere,
            anywhere,
        ],
        out_specs=vmem,
        scratch_shapes=[
            pltpu.VMEM((n, width, width), bf16),
            pltpu.VMEM((n, holds, rank, width), bf16),
            pltpu.VMEM((holds, rank, full), bf16),
            pltpu.VMEM((steps, n, rows, width), bf16),
            pltpu.VMEM((steps, rows, width), jnp.float32),
            pltpu.VMEM((rows, holds * rank), jnp.float32),
            pltpu.VMEM((steps, rows, n * CAP), bf16),
            pltpu.VMEM((steps, n, CAP, width), bf16),
            pltpu.VMEM((steps, n * CAP, width), bf16),
            pltpu.SemaphoreType.DMA((n,)),
            pltpu.SemaphoreType.DMA((n,)),
            pltpu.SemaphoreType.DMA,
            pltpu.SemaphoreType.DMA((steps, 2, hops, 2)),
            pltpu.SemaphoreType.DMA((steps, 2, hops, 2)),
            pltpu.SemaphoreType.DMA((steps, n)),
            pltpu.SemaphoreType.DMA((steps, n)),
        ],
        compiler_params=pltpu.CompilerParams(
            collective_id=0, has_side_effects=True, vmem_limit_bytes=VMEM_LIMIT
        ),
        cost_estimate=pl.CostEstimate(
            flops=2 * steps * rows * full * (width + holds * rank),
            bytes_accessed=2 * full * (width + 2 * holds * rank),
            transcendentals=0,
        ),
    )(
        acts,
        requested_adapter_ids,
        slot_of_adapter.reshape(1, -1),
        active_row_counts,
        base_projection_weight,
        jnp.swapaxes(adapter_down_factors, 1, 2),
        adapter_up_factors,
    )


def solution(mesh):
    placed = (
        P(None, ("groups", "rep"), "tensor"),
        P(None, "tensor"),
        P("tensor", None, None),
        P("tensor", None, None),
        P(None, ("groups", "rep")),
        P("groups"),
        P("groups"),
    )
    return jax.shard_map(
        per_device,
        mesh=mesh,
        in_specs=placed,
        out_specs=P(None, ("groups", "rep"), "tensor"),
        check_vma=False,
    )
```

profile of v0, /device:TPU:0, one launch (start us, length us, event | category | flops | bytes accessed | tf_op | source)
XLA Modules:
  0.0 69.9 jit_solution(2199263210658079046)
XLA Ops:
  0.0 68.2 %shard_map.73 = bf16[3,64,1024]{2,1,0:T(8,128)(2,1)} custom-call(bf16[3,64,1024]{2,1,0:T(8,128)(2,1)} %acts_ref.1, s32[3,64]{1,0:T(4,128)} %ids_ref.1, s32[1,32]{1,0:T(1,128)} %bitcast.3, s32[3]{0:T(128)} %counts_ref.1, bf16[8192,1024]{1,0:T(8,128)(2,1)} %w_hbm.1, bf16[4,64,8192]{2,1,0:T(8,128)(2,1)} %bitcast.2, bf16[4,64,8192]{2,1,0:T(8,128)(2,1)} %up_hbm.1), custom_call_target="tpu_custom_call" | custom-call | flops 4026531840 | bytes 25165824 | tf_op jit(solution)/shard_map/pallas_call | solution.py:300
  68.2 1.8 %copy.9 = bf16[3,64,1024]{2,1,0:T(8,128)(2,1)} copy(bf16[3,64,1024]{2,1,0:T(8,128)(2,1)} %shard_map.73) | data formatting | bytes 786432
where the time goes:
time: 70.1 us; the launch traced here: 69.9 us
  Pallas kernels  68.2 us (97%)
  local copies, waits for them, and re-layouts  1.77 us (3%)
    pallas_call x1, Pallas kernels, per_device(): pl.pallas_call(functools.partial(kernel, n), out_shape=jax.ShapeDtypeStru...  68.2 us
    unnamed x1, local copies, waits for them, and re-layouts  1.77 us

commit v1 on v0

--- a/solution.py
+++ b/solution.py
@@ -47,6 +47,7 @@
     down_hbm,
     up_hbm,
     out_ref,
+    acts_v,
     w_v,
     down_v,
     up_v,
@@ -54,8 +55,11 @@
     acc,
     low,
     scatter,
+    pick,
+    keep,
     d_send,
     d_recv,
+    own_sem,
     w_sem,
     down_sem,
     up_sem,
@@ -94,11 +98,8 @@
 
     up_copy = pltpu.make_async_copy(up_hbm, up_v, up_sem)
 
-    for slot in range(n):
-        for copy in w_copies(slot):
-            copy.start()
-    up_copy.start()
-
+    own_copy = pltpu.make_async_copy(acts_ref, acts_v, own_sem)
+    own_copy.start()
     barrier = pltpu.get_barrier_semaphore()
 
     def greet(offset, carry):
@@ -111,6 +112,8 @@
         return carry
 
     lax.fori_loop(1, n, greet, 0)
+    for copy in w_copies(0):
+        copy.start()
     pl.semaphore_wait(barrier, n - 1)
 
     def hop_copy(direction, s, hop, part):
@@ -118,10 +121,10 @@
         if hop == 0:
             src = acts_ref.at[s, at]
         else:
-            src = g.at[s, slot_of(direction, hop - 1), at]
+            src = g.at[slot_of(direction, hop - 1), s, at]
         return pltpu.make_async_remote_copy(
             src_ref=src,
-            dst_ref=g.at[s, slot_of(direction, hop), at],
+            dst_ref=g.at[slot_of(direction, hop), s, at],
             send_sem=g_send_sem.at[s, direction, hop, part],
             recv_sem=g_recv_sem.at[s, direction, hop, part],
             device_id={"tensor": ring[direction]},
@@ -130,12 +133,6 @@
 
     def travels(direction, hop, part):
         return hop < hops - 1 or (hop == hops - 1 and part == direction)
-
-    def start_first(s):
-        for part in range(2):
-            for direction in range(2):
-                if travels(direction, 0, part):
-                    hop_copy(direction, s, 0, part).start()
 
     def term_copy(s, offset):
         return pltpu.make_async_remote_copy(
@@ -147,47 +144,40 @@
             device_id_type=pl.DeviceIdType.MESH,
         )
 
-    def take_weights(s, slot):
-        @pl.when(s == 0)
-        def _():
-            for copy in w_copies(slot):
-                copy.wait()
-
-    def add_product(s, slot, block):
-        base = jnp.dot(block, w_v[slot], preferred_element_type=jnp.float32)
+    def add_low(slot, s, block):
+        at = pl.ds(s * rows, block.shape[0])
         small = lax.dot_general(
             block,
             down_v[slot].reshape(holds * rank, width),
             (((1,), (1,)), ((), ())),
             preferred_element_type=jnp.float32,
         )
-        if slot == 0:
-            acc[s] = base
-            low[...] = small
-        else:
-            acc[s] += base
-            low[...] += small
+        low[at] = small if slot == 0 else low[at] + small
+
+    def add_base(slot, block):
+        base = jnp.dot(block, w_v[slot], preferred_element_type=jnp.float32)
+        acc[...] = base if slot == 0 else acc[...] + base
 
     f32 = jnp.float32
 
     def iota(shape, dim):
         return lax.broadcasted_iota(jnp.int32, shape, dim).astype(f32)
 
-    def finish(s):
-        def arrived(offset, carry):
-            term_copy(s, offset).wait_recv()
-            return carry
-
-        lax.fori_loop(1, n, arrived, 0)
-        delta = jnp.dot(scatter[s], d_recv[s], preferred_element_type=f32)
-        out_ref[s] = (acc[s] + delta).astype(out_ref.dtype)
-
-    start_first(0)
-
-    def one_step(s, carry):
-        take_weights(s, 0)
-        add_product(s, 0, acts_ref[s])
-
+    pieces = [
+        (s, part, direction)
+        for s in range(steps)
+        for part in range(2)
+        for direction in range(2)
+    ]
+    for s, part, direction in pieces:
+        if travels(direction, 0, part):
+            hop_copy(direction, s, 0, part).start()
+    for slot in range(1, n):
+        for copy in w_copies(slot):
+            copy.start()
+    up_copy.start()
+
+    def place_rows(s, carry):
         ids_row = ids_ref[pl.ds(s, 1), :].astype(f32)
         table = table_ref[...].astype(f32)
         down_at, across = iota((rows, rows), 0), iota((rows, rows), 1)
@@ -210,45 +200,59 @@
         scatter[s] = jnp.where(
             target == iota((rows, n * CAP), 1), 1.0, 0.0
         ).astype(jnp.bfloat16)
-        pick = jnp.where(
+        pick[s] = jnp.where(
             (rank_row == iota((CAP, rows), 0)) & (owner_row == me.astype(f32)), 1.0, 0.0
         ).astype(jnp.bfloat16)
-
-        for hop in range(hops):
-            if hop == max(hops - 2, 0):
-
-                @pl.when(s + 1 < steps)
-                def _():
-                    start_first(s + 1)
-
-            for part in range(2):
-                for direction in range(2):
-                    if travels(direction, hop, part):
-                        hop_copy(direction, s, hop, part).wait_recv()
-                        if travels(direction, hop + 1, part):
-                            hop_copy(direction, s, hop + 1, part).start()
-            for slot in sorted({slot_of(0, hop), slot_of(1, hop)}):
-                take_weights(s, slot)
-                add_product(s, slot, g[s, slot])
-
         held = lax.broadcasted_iota(jnp.int32, (rows, holds * rank), 1) // rank
-        masked = jnp.where(local_col == held.astype(f32), low[...], 0.0)
+        keep[s] = jnp.where(local_col == held.astype(f32), 1.0, 0.0)
+        return carry
+
+    def await_weights(slot):
+        for copy in w_copies(slot):
+            copy.wait()
+
+    own_copy.wait()
+    await_weights(0)
+    own = acts_v[...].reshape(steps * rows, width)
+    add_base(0, own)
+    add_low(0, 0, own)
+    lax.fori_loop(0, steps, place_rows, 0)
+
+    def forward(hop, s, part, direction):
+        if travels(direction, hop, part):
+            hop_copy(direction, s, hop, part).wait_recv()
+            if travels(direction, hop + 1, part):
+                hop_copy(direction, s, hop + 1, part).start()
+
+    for hop in range(hops - 1):
+        for s, part, direction in pieces:
+            forward(hop, s, part, direction)
+        for slot in (slot_of(0, hop), slot_of(1, hop)):
+            await_weights(slot)
+            block = g[slot].reshape(steps * rows, width)
+            add_base(slot, block)
+            add_low(slot, 0, block)
+    await_weights(n - 1)
+    up_copy.wait()
+
+    for s in range(steps):
+        for part in range(2):
+            for direction in range(2):
+                forward(hops - 1, s, part, direction)
+        add_low(n - 1, s, g[n - 1, s])
+        masked = jnp.where(keep[s] > 0.5, low[pl.ds(s * rows, rows)], 0.0)
         packed = jnp.dot(
-            pick, masked.astype(jnp.bfloat16), preferred_element_type=f32
+            pick[s], masked.astype(jnp.bfloat16), preferred_element_type=f32
         ).astype(jnp.bfloat16)
 
-        @pl.when(s == 0)
-        def _():
-            up_copy.wait()
-
-        def term(device):
+        def term(device, packed=packed):
             at = pl.ds(pl.multiple_of(device * width, width), width)
             factor = up_v[:, :, at].reshape(holds * rank, width)
             return jnp.dot(packed, factor, preferred_element_type=f32).astype(
                 jnp.bfloat16
             )
 
-        def send_term(offset, carry):
+        def send_term(offset, carry, s=s, term=term):
             d_send[s, offset] = term((me + offset) % n)
             term_copy(s, offset).start()
             return carry
@@ -256,14 +260,20 @@
         lax.fori_loop(1, n, send_term, 0)
         d_recv[s, pl.ds(pl.multiple_of(me * CAP, CAP), CAP)] = term(me)
 
-        @pl.when(s > 0)
-        def _():
-            finish(s - 1)
-
+    add_base(n - 1, g[n - 1].reshape(steps * rows, width))
+
+    def finish(s, carry):
+        def arrived(offset, inner):
+            term_copy(s, offset).wait_recv()
+            return inner
+
+        lax.fori_loop(1, n, arrived, 0)
+        delta = jnp.dot(scatter[s], d_recv[s], preferred_element_type=f32)
+        base = acc[pl.ds(pl.multiple_of(s * rows, rows), rows)]
+        out_ref[s] = (base + delta).astype(out_ref.dtype)
         return carry
 
-    lax.fori_loop(0, steps, one_step, 0)
-    finish(steps - 1)
+    lax.fori_loop(0, steps, finish, 0)
 
     def drain(s, carry):
         for hop in range(hops):
@@ -301,7 +311,7 @@
         functools.partial(kernel, n),
         out_shape=jax.ShapeDtypeStruct(acts.shape, bf16),
         in_specs=[
-            vmem,
+            anywhere,
             vmem,
             vmem,
             pl.BlockSpec(memory_space=pltpu.SMEM),
@@ -311,15 +321,19 @@
         ],
         out_specs=vmem,
         scratch_shapes=[
+            pltpu.VMEM((steps, rows, width), bf16),
             pltpu.VMEM((n, width, width), bf16),
             pltpu.VMEM((n, holds, rank, width), bf16),
             pltpu.VMEM((holds, rank, full), bf16),
-            pltpu.VMEM((steps, n, rows, width), bf16),
-            pltpu.VMEM((steps, rows, width), jnp.float32),
-            pltpu.VMEM((rows, holds * rank), jnp.float32),
+            pltpu.VMEM((n, steps, rows, width), bf16),
+            pltpu.VMEM((steps * rows, width), jnp.float32),
+            pltpu.VMEM((steps * rows, holds * rank), jnp.float32),
             pltpu.VMEM((steps, rows, n * CAP), bf16),
+            pltpu.VMEM((steps, CAP, rows), bf16),
+            pltpu.VMEM((steps, rows, holds * rank), jnp.float32),
             pltpu.VMEM((steps, n, CAP, width), bf16),
             pltpu.VMEM((steps, n * CAP, width), bf16),
+            pltpu.SemaphoreType.DMA,
             pltpu.SemaphoreType.DMA((n,)),
             pltpu.SemaphoreType.DMA((n,)),
             pltpu.SemaphoreType.DMA,

time: 70.1 us -> 57.9 us (0.83)
  Pallas kernels: 68.2 us -> 55.9 us
    pallas_call x1, Pallas kernels: 68.2 us -> 55.9 us  [per_device(): pl.pallas_call(functools.partial(kernel, n), out_shape=jax.ShapeDtypeStru...]
where the time goes in v1:
time: 57.9 us; the launch traced here: 57.7 us
  Pallas kernels  55.9 us (97%)
  local copies, waits for them, and re-layouts  1.77 us (3%)
    pallas_call x1, Pallas kernels, per_device(): pl.pallas_call(functools.partial(kernel, n), out_shape=jax.ShapeDtypeStru...  55.9 us
    unnamed x1, local copies, waits for them, and re-layouts  1.77 us

profile of v1, /device:TPU:0, one launch (start us, length us, event | category | flops | bytes accessed | tf_op | source)
XLA Modules:
  0.0 57.7 jit_solution(3472483278350381714)
XLA Ops:
  0.0 55.9 %shard_map.73 = bf16[3,64,1024]{2,1,0:T(8,128)(2,1)} custom-call(bf16[3,64,1024]{2,1,0:T(8,128)(2,1)} %acts_ref.1, s32[3,64]{1,0:T(4,128)} %ids_ref.1, s32[1,32]{1,0:T(1,128)} %bitcast.3, s32[3]{0:T(128)} %counts_ref.1, bf16[8192,1024]{1,0:T(8,128)(2,1)} %w_hbm.1, bf16[4,64,8192]{2,1,0:T(8,128)(2,1)} %bitcast.2, bf16[4,64,8192]{2,1,0:T(8,128)(2,1)} %up_hbm.1), custom_call_target="tpu_custom_call" | custom-call | flops 4026531840 | bytes 25165824 | tf_op jit(solution)/shard_map/pallas_call | solution.py:310
  55.9 1.8 %copy.9 = bf16[3,64,1024]{2,1,0:T(8,128)(2,1)} copy(bf16[3,64,1024]{2,1,0:T(8,128)(2,1)} %shard_map.73) | data formatting | bytes 786432
